TPU v7x, 32 devices: a whole 2x2x4 slice. The times are simulated.
32 devices in a mesh: grp: 4 (over y, x), sub: 8 (over z, core).
Axes of the slice: x: 2, y: 2, z: 4, core: 2. Of those that a mesh axis runs over, the one named last changes fastest.
Arguments:
- solution: float32 [4, 8, 16, 512], P('grp', 'sub'), may hold values from -6 to 6
- residual: float32 [4, 8, 16, 512], P('grp', 'sub'), as said below
- direction: float32 [4, 8, 16, 512], P('grp', 'sub'), as said below
- inner_old: float32 [16], replicated, may hold values from 0.5 to 2
- interior: bfloat16 [4, 8, 16, 1536], P('grp', 'sub'), may hold values from -6 to 6
- weights: float32 [4, 8, 512], P('grp', 'sub'), as said below
- neighbours: int32 [4, 8, 4], P('grp', 'sub'), may hold values from -1 to 7, as said below
- coarse_rows: int32 [4, 8, 12], P('grp', 'sub'), may hold values from -1 to 119, as said below
- coarse_basis_matrix: float32 [4, 8, 12, 512], P('grp', 'sub'), may hold values from -0.5 to 0.5
- local_solver: bfloat16 [4, 8, 512, 512], P('grp', 'sub'), as said below
- schur_matrix: bfloat16 [4, 8, 512, 512], P('grp', 'sub'), as said below
- extension_values: bfloat16 [4, 8, 12, 2, 128, 128], P('grp', 'sub'), may hold values from -0.375 to 0.375
- extension_block_index: int32 [4, 8, 12, 2], P('grp', 'sub'), may hold values from 0 to 3
- coarse_inverse: float32 [120, 120], P('sub'), as said below
Outputs:
- solution_new: float32 [4, 8, 16, 512], P('grp', 'sub')
- residual_new: float32 [4, 8, 16, 512], P('grp', 'sub')
- direction_new: float32 [4, 8, 16, 512], P('grp', 'sub')
- interior_new: bfloat16 [4, 8, 16, 1536], P('grp', 'sub')
- inner_new: float32 [16], replicated
Inputs may be any that keep to these rules, and one draw needn't show every extreme that they name: Within a group the relation is symmetric: if neighbours[g, s, k] = t >= 0 then neighbours[g, t, k XOR 1] = s; the neighbours of one subdomain are distinct; -1 marks an absent block. `coarse_rows`: both subdomains of a shared face block list the same 3 rows for it, each coarse row is named by exactly two entries, and absent blocks hold -1. On a shared face the two sides' weights add up to 1; absent blocks hold 0. `residual`: equal on the two sides of every shared face, 0 on absent blocks. `direction`: equal on the two sides of every shared face, 0 on absent blocks. `local_solver`: Symmetric, with a positive diagonal larger than the sum of the magnitudes of its row's other entries. `schur_matrix`: Symmetric, with a positive diagonal larger than the sum of the magnitudes of its row's other entries. `coarse_inverse`: symmetric positive definite.
All inputs are finite; a program needn't handle non-finite values.
Results may differ from a plain program's by a relative error of at most 0.0019.
The roundings to bfloat16 on the way count: a program that leaves them out, or rounds other values in their place, can miss the bound.
Values sent between devices are 32-bit elements; how exact they have to be, the bound alone decides.
A program may use at most 64 MiB of HBM per device.

v0:
```python
import jax
import jax.numpy as jnp
from jax import lax
from jax.sharding import PartitionSpec as P

PRECISE = lax.Precision.HIGHEST


def contract(former, latter, former_dim, latter_dim):
    return lax.dot_general(
        former, latter, (((former_dim,), (latter_dim,)), ((), ())), precision=PRECISE
    )


def outgoing(blocks, neighbour, peer_count):
    active = (neighbour >= 0).astype(jnp.float32)
    clipped = jnp.maximum(neighbour, 0)
    outbound = jnp.transpose(blocks * active[None, :, None], (1, 0, 2))
    buffer = jnp.zeros((peer_count, blocks.shape[0], blocks.shape[2]), jnp.float32)
    return buffer.at[clipped].add(outbound)


def incoming(received, neighbour):
    active = (neighbour >= 0).astype(jnp.float32)
    picked = jnp.take(received, jnp.maximum(neighbour, 0), axis=0)
    return jnp.transpose(picked, (1, 0, 2)) * active[None, :, None]


def per_device(
    solution,
    residual,
    direction,
    inner_old,
    interior,
    weights,
    neighbours,
    coarse_rows,
    coarse_basis_matrix,
    local_solver,
    schur_matrix,
    extension_values,
    extension_block_index,
    coarse_inverse,
):
    peer_count = lax.axis_size("sub")
    rhs_count = residual.shape[2]
    local_faces = residual.shape[3]
    neighbour = neighbours[0, 0]
    slot_count = neighbour.shape[0]
    block_size = local_faces // slot_count
    active = jnp.repeat((neighbour >= 0).astype(jnp.float32), block_size)
    current = residual[0, 0]
    weight = weights[0, 0]
    basis_rows = coarse_basis_matrix[0, 0]
    primal = coarse_rows[0, 0]
    coarse_count = coarse_inverse.shape[1]
    face_total = coarse_count // (primal.shape[0] // slot_count) * block_size
    scaled = weight[None, :] * current
    local_solve = jnp.dot(
        scaled.astype(jnp.bfloat16), local_solver[0, 0], preferred_element_type=jnp.float32
    )
    coarse_part = contract(scaled, basis_rows, 1, 1)
    columns = lax.broadcasted_iota(jnp.int32, (primal.shape[0], coarse_count), 1)
    selector = (primal[:, None] == columns).astype(jnp.float32)
    partial_sum = jnp.dot(coarse_part, selector, precision=PRECISE)
    coarse_total = lax.psum(partial_sum, ("grp", "sub"))
    own_solution = contract(coarse_inverse, coarse_total, 1, 1)
    coarse_solution = lax.all_gather(own_solution, "sub", axis=0, tiled=True)
    coarse_local = jnp.dot(selector, coarse_solution, precision=PRECISE)
    correction = contract(coarse_local, basis_rows, 0, 0)
    weighted = weight[None, :] * (local_solve + correction)
    blocks_out = weighted.reshape(rhs_count, slot_count, block_size)
    received = lax.all_to_all(
        outgoing(blocks_out, neighbour, peer_count), "sub", split_axis=0, concat_axis=0, tiled=True
    )
    precond = weighted + incoming(received, neighbour).reshape(rhs_count, local_faces)
    inner_now = lax.psum(jnp.sum(current * precond, axis=1), ("grp", "sub")) / (2.0 * face_total)
    direction_new = precond + (inner_now / inner_old)[:, None] * direction[0, 0]
    direction_half = direction_new.astype(jnp.bfloat16)
    local_image = jnp.dot(direction_half, schur_matrix[0, 0], preferred_element_type=jnp.float32)
    image_blocks = local_image.reshape(rhs_count, slot_count, block_size)
    received_image = lax.all_to_all(
        outgoing(image_blocks, neighbour, peer_count),
        "sub",
        split_axis=0,
        concat_axis=0,
        tiled=True,
    )
    image_sum = active[None, :] * (
        local_image + incoming(received_image, neighbour).reshape(rhs_count, local_faces)
    )
    curve_term = 0.5 * jnp.sum(direction_new * image_sum, axis=1)
    curvature = lax.psum(curve_term, ("grp", "sub")) / face_total
    step_size = inner_now / curvature
    solution_new = solution[0, 0] + step_size[:, None] * direction_new
    residual_new = current - step_size[:, None] * image_sum
    direction_blocks = direction_half.reshape(rhs_count, slot_count, block_size)
    picked = jnp.take(direction_blocks, extension_block_index[0, 0], axis=1)
    extended = jnp.einsum(
        "rbjk,bjkl->rbl", picked, extension_values[0, 0], preferred_element_type=jnp.float32
    )
    extended = extended.reshape(rhs_count, -1)
    interior_new = (interior[0, 0].astype(jnp.float32) + step_size[:, None] * extended).astype(
        jnp.bfloat16
    )
    return (
        solution_new[None, None],
        residual_new[None, None],
        direction_new[None, None],
        interior_new[None, None],
        inner_now,
    )


def solution(mesh):
    in_specs = (
        P("grp", "sub", None, None),
        P("grp", "sub", None, None),
        P("grp", "sub", None, None),
        P(),
        P("grp", "sub", None, None),
        P("grp", "sub", None),
        P("grp", "sub", None),
        P("grp", "sub", None),
        P("grp", "sub", None, None),
        P("grp", "sub", None, None),
        P("grp", "sub", None, None),
        P("grp", "sub", None, None, None, None),
        P("grp", "sub", None, None),
        P("sub", None),
    )
    out_specs = (
        P("grp", "sub", None, None),
        P("grp", "sub", None, None),
        P("grp", "sub", None, None),
        P("grp", "sub", None, None),
        P(),
    )
    return jax.shard_map(
        per_device, mesh=mesh, in_specs=in_specs, out_specs=out_specs, check_vma=False
    )
```

profile of v0, /device:TPU:0, one launch (start us, length us, event | category | flops | bytes accessed | tf_op | source)
XLA Modules:
  0.0 168.9 jit_solution(9950449269539070436)
XLA Ops:
  0.6 0.0 copy-start
  0.6 0.0 copy-start.14
  0.7 0.7 fusion.35
  1.4 0.7 copy-done.8
  2.1 0.9 fusion.14
  3.0 0.0 copy-start.11
  3.0 0.7 copy-done.11
  3.7 0.2 fusion.32
  3.9 42.0 %psum.21 = f32[16,120]{1,0:T(8,128)S(1)} all-reduce(f32[16,120]{1,0:T(8,128)S(1)} %fusion.32), channel_id=1, replica_groups=mesh['grp'=4,'sub'=8] {'grp','sub'}, use_global_device_ids=true, to_apply=%region_0.0 | all-reduce | flops 1920 | bytes 15360 | tf_op jit(solution)/shard_map/psum | solution.py:66
  45.9 0.1 convolution_bitcast_fusion.1
  46.0 0.1 copy.35
  46.1 1.2 fusion.4
  47.3 14.1 %all-gather = f32[8,15,16]{2,1,0:T(8,128)S(1)} all-gather(f32[1,15,16]{2,1,0:T(8,128)S(1)} %copy.35), channel_id=1, replica_groups=mesh['grp'=4,'sub'=8] {'sub'}, dimensions={0}, use_global_device_ids=true | all-gather | bytes 8640 | tf_op jit(solution)/shard_map/all_gather | solution.py:68
  61.4 0.2 fusion.31
  61.6 0.3 fusion
  61.9 0.1 fusion.12
  62.0 0.6 broadcast.107.clone
  62.6 2.0 %scatter_fusion = f32[8,16,128]{2,1,0:T(8,128)} fusion(f32[8,16,128]{2,1,0:T(8,128)} %broadcast.107.clone, s32[4]{0:T(128)S(1)} %maximum_bitcast_fusion, f32[4,16,128]{2,1,0:T(8,128)S(1)} %fusion.12), kind=kCustom, calls=%fused_computation.3 | custom fusion | flops 8192 | bytes 98320 | tf_op jit(solution)/shard_map/scatter-add | solution.py:20
  64.5 3.6 %all-to-all-start = ((f32[8,16,128]{2,1,0:T(8,128)}), f32[8,16,128]{2,1,0:T(8,128)S(1)}, u32[]{:S(2)}, u32[]{:S(2)}) async-start(f32[8,16,128]{2,1,0:T(8,128)} %scatter_fusion), calls=%async_computation | async-start | bytes 131072 | tf_op jit(solution)/shard_map/all_to_all | solution.py:73
  68.1 0.0 copy-done.10
  68.2 0.1 broadcast_bitcast_fusion
  68.3 0.1 copy.42
  68.4 0.1 reshape.161
  68.5 5.6 %all-to-all-done = f32[8,16,128]{2,1,0:T(8,128)S(1)} async-done(((f32[8,16,128]{2,1,0:T(8,128)}), f32[8,16,128]{2,1,0:T(8,128)S(1)}, u32[]{:S(2)}, u32[]{:S(2)}) %all-to-all-start) | async-done | bytes 65568 | tf_op jit(solution)/shard_map/all_to_all | solution.py:73
  74.1 0.5 gather_fusion.1
  74.6 0.0 copy-start.7
  74.6 0.2 fusion.20
  74.8 0.1 copy.41
  74.9 39.3 %psum.22 = f32[16]{0:T(128)S(1)} all-reduce(f32[16]{0:T(128)S(1)} %fusion.20), channel_id=1, replica_groups=mesh['grp'=4,'sub'=8] {'grp','sub'}, use_global_device_ids=true, to_apply=%region_3.5 | all-reduce | flops 16 | bytes 128 | tf_op jit(solution)/shard_map/psum | solution.py:77
  114.2 0.0 copy-done.12
  114.2 0.1 convert_bitcast_fusion
  114.3 0.0 copy-start.2
  114.4 0.2 fusion.2
  114.5 0.1 fusion.11
  114.6 0.6 broadcast.107
  115.2 2.0 %scatter_fusion.1 = f32[8,16,128]{2,1,0:T(8,128)} fusion(f32[8,16,128]{2,1,0:T(8,128)} %broadcast.107, s32[4]{0:T(128)S(1)} %maximum_bitcast_fusion, f32[4,16,128]{2,1,0:T(8,128)S(1)} %fusion.11), kind=kCustom, calls=%fused_computation.4 | custom fusion | flops 8192 | bytes 98320 | tf_op jit(solution)/shard_map/scatter-add | solution.py:20
  117.2 3.3 %all-to-all-start.1 = ((f32[8,16,128]{2,1,0:T(8,128)}), f32[8,16,128]{2,1,0:T(8,128)S(1)}, u32[]{:S(2)}, u32[]{:S(2)}) async-start(f32[8,16,128]{2,1,0:T(8,128)} %scatter_fusion.1), calls=%async_computation.1 | async-start | bytes 131072 | tf_op jit(solution)/shard_map/all_to_all | solution.py:82
  120.6 0.6 gather_fusion
  121.1 0.3 convolution_bitcast_fusion
  121.5 4.9 %all-to-all-done.1 = f32[8,16,128]{2,1,0:T(8,128)S(1)} async-done(((f32[8,16,128]{2,1,0:T(8,128)}), f32[8,16,128]{2,1,0:T(8,128)S(1)}, u32[]{:S(2)}, u32[]{:S(2)}) %all-to-all-start.1) | async-done | bytes 65568 | tf_op jit(solution)/shard_map/all_to_all | solution.py:82
  126.4 0.5 gather_fusion.2
  127.0 0.2 multiply_reduce_fusion
  127.2 0.0 copy-start.6
  127.2 40.2 %psum.23 = f32[16]{0:T(128)S(1)} all-reduce(f32[16]{0:T(128)S(1)} %broadcast_multiply_fusion), channel_id=1, replica_groups=mesh['grp'=4,'sub'=8] {'grp','sub'}, use_global_device_ids=true, to_apply=%region_6.8 | all-reduce | flops 16 | bytes 128 | tf_op jit(solution)/shard_map/psum | solution.py:93
  167.4 0.0 copy-start.5
  167.4 0.7 fusion.21
  168.1 0.1 copy-done.5
  168.2 0.7 add_convert_fusion
  (31 shorter events, 0.2 us)
Async XLA Ops:
  0.6 120.5 %copy-start = (bf16[1,1,12,2,128,128]{5,4,3,2,1,0:T(8,128)(2,1)S(1)}, bf16[1,1,12,2,128,128]{5,4,3,2,1,0:T(8,128)(2,1)}, u32[]{:S(2)}) copy-start(bf16[1,1,12,2,128,128]{5,4,3,2,1,0:T(8,128)(2,1)} %param.27) | copy-start | bytes 2359300
  0.6 0.7 copy-start.14
  1.4 0.7 copy-start.8
  3.0 0.7 copy-start.11
  3.7 42.2 %copy-start.9 = (f32[15,120]{1,0:T(8,128)S(1)}, f32[15,120]{1,0:T(8,128)}, u32[]{:S(2)}) copy-start(f32[15,120]{1,0:T(8,128)} %param.29) | copy-start | bytes 21604
  3.9 42.3 %copy-start.1 = (f32[1,1,16,512]{3,2,1,0:T(8,128)S(1)}, f32[1,1,16,512]{3,2,1,0:T(8,128)}, u32[]{:S(2)}) copy-start(f32[1,1,16,512]{3,2,1,0:T(8,128)} %param.17) | copy-start | bytes 98308
  47.3 14.3 %copy-start.4 = (f32[1,1,12,512]{3,1,2,0:T(1,128)S(1)}, f32[1,1,12,512]{3,1,2,0:T(1,128)}, u32[]{:S(2)}) copy-start(f32[1,1,12,512]{3,1,2,0:T(1,128)} %param.24) | copy-start | bytes 73732
  61.4 52.9 %copy-start.3 = (bf16[1,1,512,512]{3,2,1,0:T(8,128)(2,1)S(1)}, bf16[1,1,512,512]{3,2,1,0:T(8,128)(2,1)}, u32[]{:S(2)}) copy-start(bf16[1,1,512,512]{3,2,1,0:T(8,128)(2,1)} %param.26) | copy-start | bytes 1572868
  64.5 3.6 %copy-start.10 = (s32[1,1,12,2]{2,3,1,0:T(2,128)S(1)}, s32[1,1,12,2]{2,3,1,0:T(2,128)}, u32[]{:S(2)}) copy-start(s32[1,1,12,2]{2,3,1,0:T(2,128)} %param.28) | copy-start | bytes 292
  64.5 9.5 %all-to-all-start = ((f32[8,16,128]{2,1,0:T(8,128)}), f32[8,16,128]{2,1,0:T(8,128)S(1)}, u32[]{:S(2)}, u32[]{:S(2)}) async-start(f32[8,16,128]{2,1,0:T(8,128)} %scatter_fusion), calls=%async_computation | async-start | bytes 131072 | tf_op jit(solution)/shard_map/all_to_all | solution.py:73
  74.6 39.6 %copy-start.7 = (f32[1,1,16,512]{3,2,1,0:T(8,128)S(1)}, f32[1,1,16,512]{3,2,1,0:T(8,128)}, u32[]{:S(2)}) copy-start(f32[1,1,16,512]{3,2,1,0:T(8,128)} %param.18) | copy-start | bytes 98308
  74.9 39.3 %copy-start.12 = (f32[16]{0:T(128)S(1)}, f32[16]{0:T(128)}, u32[]{:S(2)}) copy-start(f32[16]{0:T(128)} %param.19) | copy-start | bytes 196
  114.2 53.2 %copy-start.13 = (f32[16]{0:T(128)}, f32[16]{0:T(128)S(1)}, u32[]{:S(2)}) copy-start(f32[16]{0:T(128)S(1)} %get-tuple-element.9) | copy-start | bytes 196
  114.3 53.1 %copy-start.2 = (f32[16,512]{1,0:T(8,128)}, f32[16,512]{1,0:T(8,128)S(1)}, u32[]{:S(2)}) copy-start(f32[16,512]{1,0:T(8,128)S(1)} %get-tuple-element.7) | copy-start | bytes 98308
  117.2 9.2 %all-to-all-start.1 = ((f32[8,16,128]{2,1,0:T(8,128)}), f32[8,16,128]{2,1,0:T(8,128)S(1)}, u32[]{:S(2)}, u32[]{:S(2)}) async-start(f32[8,16,128]{2,1,0:T(8,128)} %scatter_fusion.1), calls=%async_computation.1 | async-start | bytes 131072 | tf_op jit(solution)/shard_map/all_to_all | solution.py:82
  127.2 40.2 %copy-start.6 = (f32[1,1,16,512]{3,2,1,0:T(8,128)S(1)}, f32[1,1,16,512]{3,2,1,0:T(8,128)}, u32[]{:S(2)}) copy-start(f32[1,1,16,512]{3,2,1,0:T(8,128)} %param.16) | copy-start | bytes 98308
  167.4 0.8 copy-start.5
where the time goes:
time: 170 us; the launch traced here: 169 us
  blocking collectives  136 us (80%)
  waiting for transfers between devices  10.5 us (6%)
  starting transfers between devices  6.94 us (4%)
  other arithmetic  6.73 us (4%)
  local copies, waits for them, and re-layouts  4.94 us (3%)
  matrix products  3.31 us (2%)
    psum x1, blocking collectives, per_device(): coarse_total = lax.psum(partial_sum, ('grp', 'sub'))  42 us
    psum x1, blocking collectives, per_device(): curvature = lax.psum(curve_term, ('grp', 'sub')) / face_total  40.2 us
    psum x1, blocking collectives, per_device(): lax.psum(jnp.sum(current * precond, axis=1), ('grp', 'sub'))  39.3 us
    all_gather x1, blocking collectives, per_device(): coarse_solution = lax.all_gather(own_solution, 'sub', axis=0, tiled=True)  14.1 us
    all_to_all x1, waiting for transfers between devices, per_device(): lax.all_to_all(outgoing(blocks_out, neighbour, peer_count), 'sub', split_...  5.6 us
    all_to_all x1, waiting for transfers between devices, per_device(): lax.all_to_all(outgoing(image_blocks, neighbour, peer_count), 'sub', spli...  4.94 us
    scatter-add x2, other arithmetic, outgoing(): return buffer.at[clipped].add(outbound)  3.91 us
    all_to_all x1, starting transfers between devices, per_device(): lax.all_to_all(outgoing(blocks_out, neighbour, peer_count), 'sub', split_...  3.59 us
  transfers between devices with their start and end apart: 2, of which 2 were waited for; matrix products, arithmetic and copies ran while one was open for 1% of the time, Pallas kernels for 0%

commit v1 on v0

--- a/solution.py
+++ b/solution.py
@@ -1,7 +1,17 @@
+import functools
+
 import jax
 import jax.numpy as jnp
 from jax import lax
+from jax.experimental import pallas as pl
+from jax.experimental.pallas import tpu as pltpu
 from jax.sharding import PartitionSpec as P
+
+MESH = pl.DeviceIdType.MESH
+LANES = 128
+SUBLANES = 8
+FIELD = 16
+COARSE_LIMIT = 128
 
 PRECISE = lax.Precision.HIGHEST
 
@@ -26,7 +36,7 @@
     return jnp.transpose(picked, (1, 0, 2)) * active[None, :, None]
 
 
-def per_device(
+def staged(
     solution,
     residual,
     direction,
@@ -112,6 +122,485 @@
     )
 
 
+def pieces(values):
+    high = values.astype(jnp.bfloat16)
+    rest = values - high.astype(jnp.float32)
+    middle = rest.astype(jnp.bfloat16)
+    low = (rest - middle.astype(jnp.float32)).astype(jnp.bfloat16)
+    return high, middle, low
+
+
+def fused_kernel(
+    n_grp,
+    n_sub,
+    face_total,
+    neighbours,
+    coarse_rows,
+    extension_index,
+    solution_in,
+    residual_in,
+    direction_in,
+    inner_old,
+    interior_in,
+    weights_in,
+    basis_in,
+    solver_in,
+    schur_in,
+    extension_in,
+    inverse_in,
+    solution_out,
+    residual_out,
+    direction_out,
+    interior_out,
+    inner_out,
+    solution_v,
+    residual_v,
+    direction_v,
+    interior_v,
+    weights_v,
+    basis_v,
+    solver_v,
+    schur_v,
+    extension_v,
+    slab_v,
+    inverse_v,
+    half_v,
+    extended_v,
+    basis_send,
+    basis_recv,
+    slab_recv,
+    packet_send,
+    packet_recv,
+    solve_send,
+    solve_recv,
+    image_send,
+    image_recv,
+    curve_send,
+    curve_recv,
+    local_sems,
+    group_send_sems,
+    group_recv_sems,
+    all_send_sems,
+    all_recv_sems,
+):
+    n_all = n_grp * n_sub
+    me_grp = lax.axis_index("grp")
+    me_sub = lax.axis_index("sub")
+    me = me_grp * n_sub + me_sub
+    cases = residual_v.shape[0]
+    slots = neighbours.shape[2]
+    primal = coarse_rows.shape[2]
+    coarse = inverse_v.shape[0]
+
+    locals_ = {}
+    for spot, (name, source, target) in enumerate(
+        (
+            ("weights", weights_in.at[0], weights_v),
+            ("residual", residual_in.at[0, 0], residual_v),
+            ("basis", basis_in.at[0, 0], basis_v),
+            ("slab", inverse_in, slab_v),
+            ("solver", solver_in.at[0, 0], solver_v),
+            ("direction", direction_in.at[0, 0], direction_v),
+            ("schur", schur_in.at[0, 0], schur_v),
+            ("extension", extension_in.at[0, 0], extension_v),
+            ("solution", solution_in.at[0, 0], solution_v),
+            ("interior", interior_in.at[0, 0], interior_v),
+        )
+    ):
+        locals_[name] = pltpu.make_async_copy(source, target, local_sems.at[spot])
+    for copy in locals_.values():
+        copy.start()
+
+    barrier = pltpu.get_barrier_semaphore()
+
+    def greet(off, carry):
+        peer = lax.rem(me + off, n_all)
+        pl.semaphore_signal(
+            barrier, inc=1, device_id=(peer // n_sub, lax.rem(peer, n_sub)), device_id_type=MESH
+        )
+        return carry
+
+    lax.fori_loop(1, n_all, greet, 0)
+
+    def group_copy(kind, off, source, target):
+        peer = lax.rem(me_sub + off, n_sub)
+        return pltpu.make_async_remote_copy(
+            src_ref=source,
+            dst_ref=target.at[me_sub],
+            send_sem=group_send_sems.at[kind, peer],
+            recv_sem=group_recv_sems.at[kind, me_sub],
+            device_id=(me_grp, peer),
+            device_id_type=MESH,
+        )
+
+    def group_arrival(kind, off, source, target):
+        peer = lax.rem(me_sub + off, n_sub)
+        return pltpu.make_async_remote_copy(
+            src_ref=source,
+            dst_ref=target.at[peer],
+            send_sem=group_send_sems.at[kind, peer],
+            recv_sem=group_recv_sems.at[kind, peer],
+            device_id=(me_grp, peer),
+            device_id_type=MESH,
+        )
+
+    def all_copy(kind, off, source, target):
+        peer = lax.rem(me + off, n_all)
+        return pltpu.make_async_remote_copy(
+            src_ref=source,
+            dst_ref=target.at[me],
+            send_sem=all_send_sems.at[kind, peer],
+            recv_sem=all_recv_sems.at[kind, me],
+            device_id=(peer // n_sub, lax.rem(peer, n_sub)),
+            device_id_type=MESH,
+        )
+
+    def all_arrival(kind, off, source, target):
+        peer = lax.rem(me + off, n_all)
+        return pltpu.make_async_remote_copy(
+            src_ref=source,
+            dst_ref=target.at[peer],
+            send_sem=all_send_sems.at[kind, peer],
+            recv_sem=all_recv_sems.at[kind, peer],
+            device_id=(peer // n_sub, lax.rem(peer, n_sub)),
+            device_id_type=MESH,
+        )
+
+    def over_all(make, act, kind, source, target):
+        def one(off, carry):
+            act(make(kind, off, source, target))
+            return carry
+
+        lax.fori_loop(1, n_all, one, 0)
+
+    beside = [neighbours[0, 0, k] for k in range(slots)]
+
+    def routed(off, blocks):
+        peer = lax.rem(me_sub + off, n_sub)
+        total = None
+        for k in range(slots):
+            term = jnp.where(beside[k] == peer, blocks[k], 0.0)
+            total = term if total is None else total + term
+        return total
+
+    def partner(received, k):
+        block = received[jnp.maximum(beside[k], 0)]
+        return jnp.where(beside[k] >= 0, block, 0.0)
+
+    def cut(values):
+        return [values[:, k * LANES : (k + 1) * LANES] for k in range(slots)]
+
+    lane = lax.broadcasted_iota(jnp.int32, (1, LANES), 1)
+    rows = jnp.full((1, LANES), -1.0, jnp.float32)
+    for m in range(primal):
+        rows = jnp.where(
+            lax.rem(lane, FIELD) == m, coarse_rows[0, 0, m].astype(jnp.float32), rows
+        )
+    locals_["weights"].wait()
+    locals_["residual"].wait()
+    locals_["basis"].wait()
+    weight = weights_v[...]
+    residual = residual_v[...]
+    scaled = weight * residual
+    basis = jnp.concatenate(
+        [basis_v[...], jnp.zeros((FIELD - primal, basis_v.shape[1]), jnp.float32)], axis=0
+    )
+    weighted_basis = weight * basis
+    sub_field = lax.broadcasted_iota(jnp.int32, (FIELD, LANES), 0)
+    basis_blocks = [jnp.where(sub_field == primal, rows, block) for block in cut(weighted_basis)]
+    for off in range(1, n_sub):
+        basis_send[off] = routed(off, basis_blocks)
+    locals_["slab"].wait()
+    slab_recv[me_sub] = slab_v[...]
+
+    pl.semaphore_wait(barrier, n_all - 1)
+    for off in range(1, n_sub):
+        group_copy(0, off, basis_send.at[off], basis_recv).start()
+        group_copy(1, off, slab_v, slab_recv).start()
+
+    locals_["solver"].wait()
+    solve = jnp.dot(
+        scaled.astype(jnp.bfloat16), solver_v[...], preferred_element_type=jnp.float32
+    )
+    wide_basis = jnp.concatenate([basis] * (LANES // FIELD), axis=0)
+    part = contract(scaled, wide_basis, 1, 1)
+    own_dot = jnp.sum(scaled * solve, axis=1, keepdims=True)
+    wide_lane = lax.broadcasted_iota(jnp.int32, (cases, LANES), 1)
+    wide_case = lax.broadcasted_iota(jnp.int32, (cases, LANES), 0)
+    part = jnp.where(lax.rem(wide_lane, FIELD) == primal, own_dot, part)
+    part = jnp.where(wide_lane // FIELD == lax.rem(wide_case, SUBLANES), part, 0.0)
+    halves = cases // SUBLANES
+    packet = jnp.concatenate(
+        [
+            jnp.sum(part[a * SUBLANES : (a + 1) * SUBLANES], axis=0, keepdims=True)
+            for a in range(halves)
+        ]
+        + [rows, jnp.zeros((1, LANES), jnp.float32)],
+        axis=0,
+    )
+    packet_send[...] = packet
+    packet_recv[me] = packet
+    over_all(all_copy, lambda copy: copy.start(), 0, packet_send, packet_recv)
+    weighted_solve = cut(weight * solve)
+    for off in range(1, n_sub):
+        solve_send[off] = routed(off, weighted_solve)
+        group_copy(2, off, solve_send.at[off], solve_recv).start()
+
+    coarse_id = lax.broadcasted_iota(jnp.int32, (coarse, LANES), 0).astype(jnp.float32)
+
+    def spread(names, values):
+        chosen = jnp.where(coarse_id == names, 1.0, 0.0)[:, :FIELD].astype(jnp.bfloat16)
+        count = values.shape[1]
+        wide = jnp.dot(
+            chosen,
+            jnp.concatenate(pieces(values), axis=1),
+            preferred_element_type=jnp.float32,
+        )
+        return (wide[:, 2 * count :] + wide[:, count : 2 * count]) + wide[:, :count]
+
+    own_spread = cut(spread(rows, weighted_basis))
+    for off in range(1, n_sub):
+        group_arrival(0, off, basis_send.at[off], basis_recv).wait_recv()
+    spreads = []
+    for k in range(slots):
+        block = partner(basis_recv, k)
+        names = block[primal : primal + 1]
+        clean = jnp.where(sub_field == primal, 0.0, block)
+        spreads.append(own_spread[k] + spread(names, clean))
+    whole_spread = jnp.concatenate(spreads, axis=1)
+    for off in range(1, n_sub):
+        group_arrival(1, off, slab_v, slab_recv).wait_recv()
+    inverse_v[...] = jnp.zeros_like(inverse_v)
+    slab_rows, slab_columns = slab_v.shape
+    for p in range(n_sub):
+        inverse_v[p * slab_rows : (p + 1) * slab_rows, :slab_columns] = slab_recv[p]
+    inverse = inverse_v[...]
+
+    over_all(all_arrival, lambda copy: copy.wait_recv(), 0, packet_send, packet_recv)
+    fields = LANES // FIELD
+    tile_lane = lax.broadcasted_iota(jnp.int32, (SUBLANES, LANES), 1) // FIELD
+    tile_sub = lax.broadcasted_iota(jnp.int32, (SUBLANES, LANES), 0)
+    turned = [[] for _ in range(halves)]
+    names = []
+    for j in range(n_all // fields):
+        tile = packet_recv[j * fields : (j + 1) * fields]
+        for a in range(halves):
+            source = tile[:, a, :]
+            result = source
+            for turn in range(1, fields):
+                moved = pltpu.roll(
+                    pltpu.roll(source, turn * FIELD, 1), SUBLANES - turn, 0
+                )
+                hit = lax.rem(tile_lane - tile_sub + fields, fields) == turn
+                result = jnp.where(hit, moved, result)
+            turned[a].append(result)
+        names.append(
+            jnp.sum(
+                jnp.where(tile_lane == tile_sub, tile[:, halves, :], 0.0), axis=0, keepdims=True
+            )
+        )
+    parts = jnp.concatenate(
+        [jnp.concatenate(turned[a], axis=1) for a in range(halves)], axis=0
+    )
+    all_names = jnp.concatenate(names, axis=1)
+    width = parts.shape[1]
+    row_id = lax.broadcasted_iota(jnp.int32, (coarse, width), 0).astype(jnp.float32)
+    selector = jnp.where(row_id == all_names, 1.0, 0.0).astype(jnp.bfloat16)
+    summed = lax.dot_general(
+        jnp.concatenate(pieces(parts), axis=0),
+        selector,
+        (((1,), (1,)), ((), ())),
+        preferred_element_type=jnp.float32,
+    )
+    coarse_total = (summed[2 * cases :] + summed[cases : 2 * cases]) + summed[:cases]
+    coarse_solution = contract(coarse_total, inverse, 1, 0)
+    correction = cut(contract(coarse_solution, whole_spread, 1, 0))
+    part_lane = lax.broadcasted_iota(jnp.int32, (cases, width), 1)
+    dots = jnp.sum(
+        jnp.where(lax.rem(part_lane, FIELD) == primal, parts, 0.0), axis=1, keepdims=True
+    )
+    dots = dots + jnp.sum(coarse_total * coarse_solution, axis=1, keepdims=True)
+    inner = dots / face_total
+    case_row = lax.broadcasted_iota(jnp.int32, (cases, cases), 0)
+    case_lane = lax.broadcasted_iota(jnp.int32, (cases, cases), 1)
+    inner_out[...] = jnp.sum(jnp.where(case_row == case_lane, inner, 0.0), axis=0, keepdims=True)
+    old = jnp.sum(
+        jnp.where(case_row == case_lane, inner_old[...], 0.0), axis=1, keepdims=True
+    )
+    ratio = inner / old
+    for off in range(1, n_sub):
+        group_arrival(2, off, solve_send.at[off], solve_recv).wait_recv()
+    locals_["direction"].wait()
+    news = []
+    for k in range(slots):
+        precond = (weighted_solve[k] + partner(solve_recv, k)) + correction[k]
+        news.append(precond + ratio * direction_v[:, k * LANES : (k + 1) * LANES])
+    direction_new = jnp.concatenate(news, axis=1)
+    direction_half = direction_new.astype(jnp.bfloat16)
+    locals_["schur"].wait()
+    local_image = cut(
+        jnp.dot(direction_half, schur_v[...], preferred_element_type=jnp.float32)
+    )
+    for off in range(1, n_sub):
+        image_send[off] = routed(off, local_image)
+        group_copy(3, off, image_send.at[off], image_recv).start()
+    bent = None
+    for k in range(slots):
+        term = jnp.where(beside[k] >= 0, news[k] * local_image[k], 0.0)
+        bent = term if bent is None else bent + term
+    bent = jnp.sum(bent, axis=1, keepdims=True)
+    bent_row = jnp.sum(jnp.where(wide_lane == wide_case, bent, 0.0), axis=0, keepdims=True)
+    curve_send[...] = bent_row
+    curve_recv[me] = bent_row
+    over_all(all_copy, lambda copy: copy.start(), 1, curve_send, curve_recv)
+
+    direction_out[0, 0] = direction_new
+    for k in range(slots):
+        half_v[k] = direction_half[:, k * LANES : (k + 1) * LANES]
+    locals_["extension"].wait()
+    for b in range(extension_v.shape[0]):
+        total = None
+        for j in range(extension_v.shape[1]):
+            term = jnp.dot(
+                half_v[extension_index[0, 0, b, j]],
+                extension_v[b, j],
+                preferred_element_type=jnp.float32,
+            )
+            total = term if total is None else total + term
+        extended_v[:, b * LANES : (b + 1) * LANES] = total
+    locals_["solution"].wait()
+    locals_["interior"].wait()
+
+    over_all(all_arrival, lambda copy: copy.wait_recv(), 1, curve_send, curve_recv)
+    gathered = [curve_recv[d] for d in range(n_all)]
+    while len(gathered) > 1:
+        gathered = [
+            sum(gathered[i + 1 : i + 2], gathered[i]) for i in range(0, len(gathered), 2)
+        ]
+    curvature = (
+        jnp.sum(jnp.where(wide_lane == wide_case, gathered[0], 0.0), axis=1, keepdims=True)
+        / face_total
+    )
+    step = inner / curvature
+    solution_out[0, 0] = solution_v[...] + step * direction_new
+    interior_out[0, 0] = (
+        interior_v[...].astype(jnp.float32) + step * extended_v[...]
+    ).astype(jnp.bfloat16)
+    for off in range(1, n_sub):
+        group_arrival(3, off, image_send.at[off], image_recv).wait_recv()
+    for k in range(slots):
+        image = jnp.where(beside[k] >= 0, local_image[k] + partner(image_recv, k), 0.0)
+        span = slice(k * LANES, (k + 1) * LANES)
+        residual_out[0, 0, :, span] = residual[:, span] - step * image
+
+    for off in range(1, n_sub):
+        group_copy(0, off, basis_send.at[off], basis_recv).wait_send()
+        group_copy(1, off, slab_v, slab_recv).wait_send()
+        group_copy(2, off, solve_send.at[off], solve_recv).wait_send()
+        group_copy(3, off, image_send.at[off], image_recv).wait_send()
+    over_all(all_copy, lambda copy: copy.wait_send(), 0, packet_send, packet_recv)
+    over_all(all_copy, lambda copy: copy.wait_send(), 1, curve_send, curve_recv)
+
+
+def fused(
+    solution,
+    residual,
+    direction,
+    inner_old,
+    interior,
+    weights,
+    neighbours,
+    coarse_rows,
+    coarse_basis_matrix,
+    local_solver,
+    schur_matrix,
+    extension_values,
+    extension_block_index,
+    coarse_inverse,
+):
+    n_grp, n_sub = lax.axis_size("grp"), lax.axis_size("sub")
+    n_all = n_grp * n_sub
+    cases, faces = residual.shape[2:]
+    interior_faces = interior.shape[3]
+    slots = neighbours.shape[2]
+    primal = coarse_rows.shape[2]
+    slab_rows, coarse_count = coarse_inverse.shape
+    coarse = -(-coarse_count // LANES) * LANES
+    face_total = coarse_count // (primal // slots) * (faces // slots)
+    f32, bf16 = jnp.float32, jnp.bfloat16
+    smem = pl.BlockSpec(memory_space=pltpu.SMEM)
+    vmem = pl.BlockSpec(memory_space=pltpu.VMEM)
+    far = pl.BlockSpec(memory_space=pl.ANY)
+    outs = pl.pallas_call(
+        functools.partial(fused_kernel, n_grp, n_sub, float(face_total)),
+        out_shape=[
+            jax.ShapeDtypeStruct(solution.shape, f32),
+            jax.ShapeDtypeStruct(residual.shape, f32),
+            jax.ShapeDtypeStruct(direction.shape, f32),
+            jax.ShapeDtypeStruct(interior.shape, bf16),
+            jax.ShapeDtypeStruct((1, cases), f32),
+        ],
+        in_specs=[smem, smem, smem, far, far, far, vmem, far, far, far, far, far, far, far],
+        out_specs=[vmem] * 5,
+        scratch_shapes=[
+            pltpu.VMEM((cases, faces), f32),
+            pltpu.VMEM((cases, faces), f32),
+            pltpu.VMEM((cases, faces), f32),
+            pltpu.VMEM((cases, interior_faces), bf16),
+            pltpu.VMEM((1, faces), f32),
+            pltpu.VMEM((primal, faces), f32),
+            pltpu.VMEM((faces, faces), bf16),
+            pltpu.VMEM((faces, faces), bf16),
+            pltpu.VMEM(extension_values.shape[2:], bf16),
+            pltpu.VMEM((slab_rows, coarse_count), f32),
+            pltpu.VMEM((coarse, coarse), f32),
+            pltpu.VMEM((slots, cases, LANES), bf16),
+            pltpu.VMEM((cases, interior_faces), f32),
+            pltpu.VMEM((n_sub, FIELD, LANES), f32),
+            pltpu.VMEM((n_sub, FIELD, LANES), f32),
+            pltpu.VMEM((n_sub, slab_rows, coarse_count), f32),
+            pltpu.VMEM((cases // SUBLANES + 2, LANES), f32),
+            pltpu.VMEM((n_all, cases // SUBLANES + 2, LANES), f32),
+            pltpu.VMEM((n_sub, cases, LANES), f32),
+            pltpu.VMEM((n_sub, cases, LANES), f32),
+            pltpu.VMEM((n_sub, cases, LANES), f32),
+            pltpu.VMEM((n_sub, cases, LANES), f32),
+            pltpu.VMEM((1, LANES), f32),
+            pltpu.VMEM((n_all, 1, LANES), f32),
+            pltpu.SemaphoreType.DMA((10,)),
+            pltpu.SemaphoreType.DMA((4, n_sub)),
+            pltpu.SemaphoreType.DMA((4, n_sub)),
+            pltpu.SemaphoreType.DMA((2, n_all)),
+            pltpu.SemaphoreType.DMA((2, n_all)),
+        ],
+        compiler_params=pltpu.CompilerParams(
+            collective_id=0, has_side_effects=True, vmem_limit_bytes=24 * 1024 * 1024
+        ),
+    )(
+        neighbours,
+        coarse_rows,
+        extension_block_index,
+        solution,
+        residual,
+        direction,
+        inner_old.reshape(1, cases),
+        interior,
+        weights,
+        coarse_basis_matrix,
+        local_solver,
+        schur_matrix,
+        extension_values,
+        coarse_inverse,
+    )
+    return (*outs[:4], outs[4].reshape(cases))
+
+
+def per_device(*arrays):
+    if arrays[-1].shape[1] <= COARSE_LIMIT:
+        return fused(*arrays)
+    return staged(*arrays)
+
+
 def solution(mesh):
     in_specs = (
         P("grp", "sub", None, None),

time: 170 us -> 36 us (0.21)
  blocking collectives: 136 us -> 0 us
  Pallas kernels: 0 us -> 24.7 us
  waiting for transfers between devices: 10.5 us -> 0 us
  starting transfers between devices: 6.94 us -> 0 us
  other arithmetic: 6.73 us -> 0 us
  local copies, waits for them, and re-layouts: 4.94 us -> 10 us
  matrix products: 3.31 us -> 0 us
    psum x3 -> x0, blocking collectives: 122 us -> none  [the longest x1 42 us: per_device(): coarse_total = lax.psum(partial_sum, ('grp', 'sub'))]
    pallas_call x0 -> x1, Pallas kernels: none -> 24.7 us  [fused(): pl.pallas_call(functools.partial(fused_kernel, n_grp, n_sub, float(face_t...]
    all_gather x1 -> x0, blocking collectives: 14.1 us -> none  [per_device(): coarse_solution = lax.all_gather(own_solution, 'sub', axis=0, tiled=True)]
    all_to_all x2 -> x0, waiting for transfers between devices: 10.5 us -> none  [the longest x1 5.6 us: per_device(): lax.all_to_all(outgoing(blocks_out, neighbour, peer_count), 'sub', split_...]
    unnamed x32 -> x33, local copies, waits for them, and re-layouts: 1.58 us -> 10 us
    all_to_all x2 -> x0, starting transfers between devices: 6.94 us -> none  [the longest x1 3.59 us: per_device(): lax.all_to_all(outgoing(blocks_out, neighbour, peer_count), 'sub', split_...]
    scatter-add x2 -> x0, other arithmetic: 3.91 us -> none  [outgoing(): return buffer.at[clipped].add(outbound)]
    dot_general x8 -> x0, matrix products: 3.31 us -> none  [the longest x3 1.28 us: contract(): lax.dot_general(former, latter, (((former_dim,), (latter_dim,)), ((), ())...]
  transfers between devices with their start and end apart: 2 -> 0, of which waited for: 2 -> 0; matrix products, arithmetic and copies ran while one was open for 1% -> 0% of each run, Pallas kernels for 0% -> 0%
where the time goes in v1:
time: 36 us; the launch traced here: 35.5 us
  Pallas kernels  24.7 us (69%)
  local copies, waits for them, and re-layouts  10 us (28%)
  between operations  0.71 us (2%)
    pallas_call x1, Pallas kernels, fused(): pl.pallas_call(functools.partial(fused_kernel, n_grp, n_sub, float(face_t...  24.7 us
    unnamed x33, local copies, waits for them, and re-layouts  10 us

profile of v1, /device:TPU:0, one launch (start us, length us, event | category | flops | bytes accessed | tf_op | source)
XLA Modules:
  0.0 35.5 jit_solution(1491541591364244142)
XLA Ops:
  0.6 0.0 copy-start.12
  0.6 0.0 copy-start.3
  0.7 0.7 %copy-done.12 = s32[1,1,12,2]{2,3,1,0:T(2,128)S(1)} copy-done((s32[1,1,12,2]{2,3,1,0:T(2,128)S(1)}, s32[1,1,12,2]{2,3,1,0:T(2,128)}, u32[]{:S(2)}) %copy-start.12) | copy-done | bytes 120
  1.3 0.1 copy.19.extension_index
  1.4 0.0 copy-start.7
  1.4 0.0 copy-start.8
  1.4 0.0 copy-start.9
  1.4 0.0 copy-start.10
  1.4 0.0 copy-start.11
  1.4 0.8 %copy.20.basis_in = f32[1,1,12,512]{3,2,1,0:T(8,128)S(1)} copy(f32[1,1,12,512]{3,1,2,0:T(1,128)} %param.22) | data formatting | bytes 49152 | tf_op args[8]
  2.2 0.0 copy-done.3
  2.2 0.0 copy-done.7
  2.2 0.0 copy-done.8
  2.2 0.0 copy-done.9
  2.2 0.0 copy-done.10
  2.3 0.0 copy-done.11
  2.3 0.0 copy-start
  2.3 1.1 %copy-done = bf16[1,1,12,2,128,128]{5,4,3,2,1,0:T(8,128)(2,1)S(1)} copy-done((bf16[1,1,12,2,128,128]{5,4,3,2,1,0:T(8,128)(2,1)S(1)}, bf16[1,1,12,2,128,128]{5,4,3,2,1,0:T(8,128)(2,1)}, u32[]{:S(2)}) %copy-start) | copy-done | bytes 786456
  3.4 0.0 copy-start.1
  3.4 1.0 %copy-done.1 = bf16[1,1,512,512]{3,2,1,0:T(8,128)(2,1)S(1)} copy-done((bf16[1,1,512,512]{3,2,1,0:T(8,128)(2,1)S(1)}, bf16[1,1,512,512]{3,2,1,0:T(8,128)(2,1)}, u32[]{:S(2)}) %copy-start.1) | copy-done | bytes 524312
  4.4 0.0 copy-start.2
  4.4 1.0 %copy-done.2 = bf16[1,1,512,512]{3,2,1,0:T(8,128)(2,1)S(1)} copy-done((bf16[1,1,512,512]{3,2,1,0:T(8,128)(2,1)S(1)}, bf16[1,1,512,512]{3,2,1,0:T(8,128)(2,1)}, u32[]{:S(2)}) %copy-start.2) | copy-done | bytes 524312
  5.5 0.0 copy-start.4
  5.5 0.8 %copy-done.4 = f32[1,1,16,512]{3,2,1,0:T(8,128)S(1)} copy-done((f32[1,1,16,512]{3,2,1,0:T(8,128)S(1)}, f32[1,1,16,512]{3,2,1,0:T(8,128)}, u32[]{:S(2)}) %copy-start.4) | copy-done | bytes 32792
  6.2 0.0 copy-start.5
  6.2 0.8 %copy-done.5 = f32[1,1,16,512]{3,2,1,0:T(8,128)S(1)} copy-done((f32[1,1,16,512]{3,2,1,0:T(8,128)S(1)}, f32[1,1,16,512]{3,2,1,0:T(8,128)}, u32[]{:S(2)}) %copy-start.5) | copy-done | bytes 32792
  7.0 0.0 copy-start.6
  7.0 0.8 %copy-done.6 = f32[1,1,16,512]{3,2,1,0:T(8,128)S(1)} copy-done((f32[1,1,16,512]{3,2,1,0:T(8,128)S(1)}, f32[1,1,16,512]{3,2,1,0:T(8,128)}, u32[]{:S(2)}) %copy-start.6) | copy-done | bytes 32792
  7.8 24.7 %shard_map.173 = (f32[1,1,16,512]{3,2,1,0:T(8,128)S(1)}, f32[1,1,16,512]{3,2,1,0:T(8,128)S(1)}, f32[1,1,16,512]{3,2,1,0:T(8,128)S(1)}, bf16[1,1,16,1536]{3,2,1,0:T(8,128)(2,1)S(1)}, f32[1,16]{1,0:T(1,128)S(1)}) custom-call(s32[1,1,4]{2,1,0:T(1,128)S(1)} %copy-done.9, s32[1,1,12]{2,1,0:T(1,128)S(1)} %copy-done.10, s32[1,1,12,2]{3,2,1,0:T(8,128)S(1)} %copy.19.extension_index, ...), custom_call_target="tpu_custom_call" | custom-call | tf_op jit(solution)/shard_map/pallas_call | solution.py:534
  32.5 0.6 %copy.26 = f32[1,1,16,512]{3,2,1,0:T(8,128)} copy(f32[1,1,16,512]{3,2,1,0:T(8,128)S(1)} %get-tuple-element.20) | data formatting | bytes 65536
  33.1 0.6 %copy.27 = f32[1,1,16,512]{3,2,1,0:T(8,128)} copy(f32[1,1,16,512]{3,2,1,0:T(8,128)S(1)} %get-tuple-element.21) | data formatting | bytes 65536
  33.7 0.6 %copy.28 = f32[1,1,16,512]{3,2,1,0:T(8,128)} copy(f32[1,1,16,512]{3,2,1,0:T(8,128)S(1)} %get-tuple-element.22) | data formatting | bytes 65536
  34.3 0.6 %copy.29 = bf16[1,1,16,1536]{3,2,1,0:T(8,128)(2,1)} copy(bf16[1,1,16,1536]{3,2,1,0:T(8,128)(2,1)S(1)} %get-tuple-element.23) | data formatting | bytes 98304
  35.0 0.5 %copy.30 = f32[16]{0:T(128)} copy(f32[16]{0:T(128)S(1)} %bitcast.3) | data formatting | bytes 128
Async XLA Ops:
  0.6 0.7 %copy-start.12 = (s32[1,1,12,2]{2,3,1,0:T(2,128)S(1)}, s32[1,1,12,2]{2,3,1,0:T(2,128)}, u32[]{:S(2)}) copy-start(s32[1,1,12,2]{2,3,1,0:T(2,128)} %param.26) | copy-start | bytes 292
  0.6 1.6 %copy-start.3 = (bf16[1,1,16,1536]{3,2,1,0:T(8,128)(2,1)S(1)}, bf16[1,1,16,1536]{3,2,1,0:T(8,128)(2,1)}, u32[]{:S(2)}) copy-start(bf16[1,1,16,1536]{3,2,1,0:T(8,128)(2,1)} %interior_in.1) | copy-start | bytes 147460
  1.4 0.8 %copy-start.7 = (f32[15,120]{1,0:T(8,128)S(1)}, f32[15,120]{1,0:T(8,128)}, u32[]{:S(2)}) copy-start(f32[15,120]{1,0:T(8,128)} %inverse_in.1) | copy-start | bytes 21604
  1.4 0.8 %copy-start.8 = (f32[1,1,512]{2,1,0:T(1,128)S(1)}, f32[1,1,512]{2,1,0:T(1,128)}, u32[]{:S(2)}) copy-start(f32[1,1,512]{2,1,0:T(1,128)} %weights_in.1) | copy-start | bytes 6148
  1.4 0.8 %copy-start.9 = (s32[1,1,4]{2,1,0:T(1,128)S(1)}, s32[1,1,4]{2,1,0:T(1,128)}, u32[]{:S(2)}) copy-start(s32[1,1,4]{2,1,0:T(1,128)} %neighbours.1) | copy-start | bytes 52
  1.4 0.8 %copy-start.10 = (s32[1,1,12]{2,1,0:T(1,128)S(1)}, s32[1,1,12]{2,1,0:T(1,128)}, u32[]{:S(2)}) copy-start(s32[1,1,12]{2,1,0:T(1,128)} %coarse_rows.1) | copy-start | bytes 148
  1.4 0.8 %copy-start.11 = (f32[16]{0:T(128)S(1)}, f32[16]{0:T(128)}, u32[]{:S(2)}) copy-start(f32[16]{0:T(128)} %param.17) | copy-start | bytes 196
  2.3 1.1 %copy-start = (bf16[1,1,12,2,128,128]{5,4,3,2,1,0:T(8,128)(2,1)S(1)}, bf16[1,1,12,2,128,128]{5,4,3,2,1,0:T(8,128)(2,1)}, u32[]{:S(2)}) copy-start(bf16[1,1,12,2,128,128]{5,4,3,2,1,0:T(8,128)(2,1)} %extension_in.1) | copy-start | bytes 2359300
  3.4 1.0 %copy-start.1 = (bf16[1,1,512,512]{3,2,1,0:T(8,128)(2,1)S(1)}, bf16[1,1,512,512]{3,2,1,0:T(8,128)(2,1)}, u32[]{:S(2)}) copy-start(bf16[1,1,512,512]{3,2,1,0:T(8,128)(2,1)} %solver_in.1) | copy-start | bytes 1572868
  4.4 1.0 %copy-start.2 = (bf16[1,1,512,512]{3,2,1,0:T(8,128)(2,1)S(1)}, bf16[1,1,512,512]{3,2,1,0:T(8,128)(2,1)}, u32[]{:S(2)}) copy-start(bf16[1,1,512,512]{3,2,1,0:T(8,128)(2,1)} %schur_in.1) | copy-start | bytes 1572868
  5.5 0.8 %copy-start.4 = (f32[1,1,16,512]{3,2,1,0:T(8,128)S(1)}, f32[1,1,16,512]{3,2,1,0:T(8,128)}, u32[]{:S(2)}) copy-start(f32[1,1,16,512]{3,2,1,0:T(8,128)} %solution_in.1) | copy-start | bytes 98308
  6.2 0.8 %copy-start.5 = (f32[1,1,16,512]{3,2,1,0:T(8,128)S(1)}, f32[1,1,16,512]{3,2,1,0:T(8,128)}, u32[]{:S(2)}) copy-start(f32[1,1,16,512]{3,2,1,0:T(8,128)} %residual_in.1) | copy-start | bytes 98308
  7.0 0.8 %copy-start.6 = (f32[1,1,16,512]{3,2,1,0:T(8,128)S(1)}, f32[1,1,16,512]{3,2,1,0:T(8,128)}, u32[]{:S(2)}) copy-start(f32[1,1,16,512]{3,2,1,0:T(8,128)} %direction_in.1) | copy-start | bytes 98308

commit v2 on v1

--- a/solution.py
+++ b/solution.py
@@ -12,6 +12,7 @@
 SUBLANES = 8
 FIELD = 16
 COARSE_LIMIT = 128
+HELD_BYTES = 60 * 1024 * 1024
 
 PRECISE = lax.Precision.HIGHEST
 
@@ -134,13 +135,13 @@
     n_grp,
     n_sub,
     face_total,
-    neighbours,
-    coarse_rows,
-    extension_index,
+    neighbours_in,
+    rows_in,
+    index_in,
     solution_in,
     residual_in,
     direction_in,
-    inner_old,
+    inner_in,
     interior_in,
     weights_in,
     basis_in,
@@ -153,6 +154,11 @@
     direction_out,
     interior_out,
     inner_out,
+    neighbours,
+    coarse_rows,
+    extension_index,
+    inner_old,
+    split_v,
     solution_v,
     residual_v,
     direction_v,
@@ -178,10 +184,8 @@
     curve_send,
     curve_recv,
     local_sems,
-    group_send_sems,
-    group_recv_sems,
-    all_send_sems,
-    all_recv_sems,
+    send_sems,
+    recv_sems,
 ):
     n_all = n_grp * n_sub
     me_grp = lax.axis_index("grp")
@@ -195,11 +199,15 @@
     locals_ = {}
     for spot, (name, source, target) in enumerate(
         (
+            ("neighbours", neighbours_in, neighbours),
+            ("rows", rows_in, coarse_rows),
             ("weights", weights_in.at[0], weights_v),
             ("residual", residual_in.at[0, 0], residual_v),
-            ("basis", basis_in.at[0, 0], basis_v),
+            ("basis", basis_in.at[0], basis_v),
             ("slab", inverse_in, slab_v),
             ("solver", solver_in.at[0, 0], solver_v),
+            ("inner", inner_in, inner_old),
+            ("index", index_in, extension_index),
             ("direction", direction_in.at[0, 0], direction_v),
             ("schur", schur_in.at[0, 0], schur_v),
             ("extension", extension_in.at[0, 0], extension_v),
@@ -213,70 +221,49 @@
 
     barrier = pltpu.get_barrier_semaphore()
 
-    def greet(off, carry):
-        peer = lax.rem(me + off, n_all)
-        pl.semaphore_signal(
-            barrier, inc=1, device_id=(peer // n_sub, lax.rem(peer, n_sub)), device_id_type=MESH
-        )
-        return carry
-
-    lax.fori_loop(1, n_all, greet, 0)
+    sub_peers = [lax.rem(me_sub + off, n_sub) for off in range(n_sub)]
+    grp_peers = [lax.rem(me_grp + off, n_grp) for off in range(n_grp)]
+    everyone = [(g, s) for s in sub_peers for g in grp_peers][1:]
+    for peer in everyone:
+        pl.semaphore_signal(barrier, inc=1, device_id=peer, device_id_type=MESH)
 
     def group_copy(kind, off, source, target):
-        peer = lax.rem(me_sub + off, n_sub)
         return pltpu.make_async_remote_copy(
             src_ref=source,
             dst_ref=target.at[me_sub],
-            send_sem=group_send_sems.at[kind, peer],
-            recv_sem=group_recv_sems.at[kind, me_sub],
-            device_id=(me_grp, peer),
+            send_sem=send_sems.at[kind],
+            recv_sem=recv_sems.at[kind],
+            device_id=(me_grp, sub_peers[off]),
             device_id_type=MESH,
         )
 
-    def group_arrival(kind, off, source, target):
-        peer = lax.rem(me_sub + off, n_sub)
-        return pltpu.make_async_remote_copy(
-            src_ref=source,
-            dst_ref=target.at[peer],
-            send_sem=group_send_sems.at[kind, peer],
-            recv_sem=group_recv_sems.at[kind, peer],
-            device_id=(me_grp, peer),
-            device_id_type=MESH,
-        )
-
-    def all_copy(kind, off, source, target):
-        peer = lax.rem(me + off, n_all)
+    def all_copy(kind, peer, source, target):
         return pltpu.make_async_remote_copy(
             src_ref=source,
             dst_ref=target.at[me],
-            send_sem=all_send_sems.at[kind, peer],
-            recv_sem=all_recv_sems.at[kind, me],
-            device_id=(peer // n_sub, lax.rem(peer, n_sub)),
+            send_sem=send_sems.at[kind],
+            recv_sem=recv_sems.at[kind],
+            device_id=peer,
             device_id_type=MESH,
         )
 
-    def all_arrival(kind, off, source, target):
-        peer = lax.rem(me + off, n_all)
+    def all_of(kind, target):
+        span = target.at[pl.ds(0, target.shape[0] - 1)]
         return pltpu.make_async_remote_copy(
-            src_ref=source,
-            dst_ref=target.at[peer],
-            send_sem=all_send_sems.at[kind, peer],
-            recv_sem=all_recv_sems.at[kind, peer],
-            device_id=(peer // n_sub, lax.rem(peer, n_sub)),
+            src_ref=span,
+            dst_ref=span,
+            send_sem=send_sems.at[kind],
+            recv_sem=recv_sems.at[kind],
+            device_id=everyone[0],
             device_id_type=MESH,
         )
 
-    def over_all(make, act, kind, source, target):
-        def one(off, carry):
-            act(make(kind, off, source, target))
-            return carry
-
-        lax.fori_loop(1, n_all, one, 0)
-
+    locals_["neighbours"].wait()
+    locals_["rows"].wait()
     beside = [neighbours[0, 0, k] for k in range(slots)]
 
     def routed(off, blocks):
-        peer = lax.rem(me_sub + off, n_sub)
+        peer = sub_peers[off]
         total = None
         for k in range(slots):
             term = jnp.where(beside[k] == peer, blocks[k], 0.0)
@@ -303,13 +290,21 @@
     residual = residual_v[...]
     scaled = weight * residual
     basis = jnp.concatenate(
-        [basis_v[...], jnp.zeros((FIELD - primal, basis_v.shape[1]), jnp.float32)], axis=0
+        [basis_v[m] for m in range(primal)]
+        + [jnp.zeros((FIELD - primal, basis_v.shape[2]), jnp.float32)],
+        axis=0,
     )
     weighted_basis = weight * basis
     sub_field = lax.broadcasted_iota(jnp.int32, (FIELD, LANES), 0)
     basis_blocks = [jnp.where(sub_field == primal, rows, block) for block in cut(weighted_basis)]
     for off in range(1, n_sub):
         basis_send[off] = routed(off, basis_blocks)
+    wide_lane = lax.broadcasted_iota(jnp.int32, (cases, LANES), 1)
+    wide_case = lax.broadcasted_iota(jnp.int32, (cases, LANES), 0)
+    part = jnp.zeros((cases, LANES), jnp.float32)
+    for m in range(primal):
+        column = jnp.sum(scaled * basis[m : m + 1], axis=1, keepdims=True)
+        part = jnp.where(lax.rem(wide_lane, FIELD) == m, column, part)
     locals_["slab"].wait()
     slab_recv[me_sub] = slab_v[...]
 
@@ -322,11 +317,7 @@
     solve = jnp.dot(
         scaled.astype(jnp.bfloat16), solver_v[...], preferred_element_type=jnp.float32
     )
-    wide_basis = jnp.concatenate([basis] * (LANES // FIELD), axis=0)
-    part = contract(scaled, wide_basis, 1, 1)
     own_dot = jnp.sum(scaled * solve, axis=1, keepdims=True)
-    wide_lane = lax.broadcasted_iota(jnp.int32, (cases, LANES), 1)
-    wide_case = lax.broadcasted_iota(jnp.int32, (cases, LANES), 0)
     part = jnp.where(lax.rem(wide_lane, FIELD) == primal, own_dot, part)
     part = jnp.where(wide_lane // FIELD == lax.rem(wide_case, SUBLANES), part, 0.0)
     halves = cases // SUBLANES
@@ -340,7 +331,8 @@
     )
     packet_send[...] = packet
     packet_recv[me] = packet
-    over_all(all_copy, lambda copy: copy.start(), 0, packet_send, packet_recv)
+    for peer in everyone:
+        all_copy(4, peer, packet_send, packet_recv).start()
     weighted_solve = cut(weight * solve)
     for off in range(1, n_sub):
         solve_send[off] = routed(off, weighted_solve)
@@ -359,8 +351,7 @@
         return (wide[:, 2 * count :] + wide[:, count : 2 * count]) + wide[:, :count]
 
     own_spread = cut(spread(rows, weighted_basis))
-    for off in range(1, n_sub):
-        group_arrival(0, off, basis_send.at[off], basis_recv).wait_recv()
+    all_of(0, basis_recv).wait_recv()
     spreads = []
     for k in range(slots):
         block = partner(basis_recv, k)
@@ -368,15 +359,16 @@
         clean = jnp.where(sub_field == primal, 0.0, block)
         spreads.append(own_spread[k] + spread(names, clean))
     whole_spread = jnp.concatenate(spreads, axis=1)
-    for off in range(1, n_sub):
-        group_arrival(1, off, slab_v, slab_recv).wait_recv()
+    all_of(1, slab_recv).wait_recv()
     inverse_v[...] = jnp.zeros_like(inverse_v)
     slab_rows, slab_columns = slab_v.shape
     for p in range(n_sub):
         inverse_v[p * slab_rows : (p + 1) * slab_rows, :slab_columns] = slab_recv[p]
     inverse = inverse_v[...]
-
-    over_all(all_arrival, lambda copy: copy.wait_recv(), 0, packet_send, packet_recv)
+    both = jnp.concatenate([inverse, contract(inverse, whole_spread, 1, 0)], axis=1)
+    split_v[0], split_v[1] = pieces(both)[:2]
+
+    all_of(4, packet_recv).wait_recv()
     fields = LANES // FIELD
     tile_lane = lax.broadcasted_iota(jnp.int32, (SUBLANES, LANES), 1) // FIELD
     tile_sub = lax.broadcasted_iota(jnp.int32, (SUBLANES, LANES), 0)
@@ -413,8 +405,13 @@
         preferred_element_type=jnp.float32,
     )
     coarse_total = (summed[2 * cases :] + summed[cases : 2 * cases]) + summed[:cases]
-    coarse_solution = contract(coarse_total, inverse, 1, 0)
-    correction = cut(contract(coarse_solution, whole_spread, 1, 0))
+    stacked = jnp.concatenate(pieces(coarse_total)[:2], axis=0)
+    solved = jnp.dot(stacked, split_v[0], preferred_element_type=jnp.float32) + jnp.dot(
+        stacked, split_v[1], preferred_element_type=jnp.float32
+    )
+    solved = solved[:cases] + solved[cases:]
+    coarse_solution = solved[:, :coarse]
+    correction = cut(solved[:, coarse:])
     part_lane = lax.broadcasted_iota(jnp.int32, (cases, width), 1)
     dots = jnp.sum(
         jnp.where(lax.rem(part_lane, FIELD) == primal, parts, 0.0), axis=1, keepdims=True
@@ -424,12 +421,12 @@
     case_row = lax.broadcasted_iota(jnp.int32, (cases, cases), 0)
     case_lane = lax.broadcasted_iota(jnp.int32, (cases, cases), 1)
     inner_out[...] = jnp.sum(jnp.where(case_row == case_lane, inner, 0.0), axis=0, keepdims=True)
+    locals_["inner"].wait()
     old = jnp.sum(
         jnp.where(case_row == case_lane, inner_old[...], 0.0), axis=1, keepdims=True
     )
     ratio = inner / old
-    for off in range(1, n_sub):
-        group_arrival(2, off, solve_send.at[off], solve_recv).wait_recv()
+    all_of(2, solve_recv).wait_recv()
     locals_["direction"].wait()
     news = []
     for k in range(slots):
@@ -452,17 +449,19 @@
     bent_row = jnp.sum(jnp.where(wide_lane == wide_case, bent, 0.0), axis=0, keepdims=True)
     curve_send[...] = bent_row
     curve_recv[me] = bent_row
-    over_all(all_copy, lambda copy: copy.start(), 1, curve_send, curve_recv)
+    for peer in everyone:
+        all_copy(5, peer, curve_send, curve_recv).start()
 
     direction_out[0, 0] = direction_new
     for k in range(slots):
         half_v[k] = direction_half[:, k * LANES : (k + 1) * LANES]
+    locals_["index"].wait()
     locals_["extension"].wait()
     for b in range(extension_v.shape[0]):
         total = None
         for j in range(extension_v.shape[1]):
             term = jnp.dot(
-                half_v[extension_index[0, 0, b, j]],
+                half_v[extension_index[0, 0, j, b]],
                 extension_v[b, j],
                 preferred_element_type=jnp.float32,
             )
@@ -471,7 +470,7 @@
     locals_["solution"].wait()
     locals_["interior"].wait()
 
-    over_all(all_arrival, lambda copy: copy.wait_recv(), 1, curve_send, curve_recv)
+    all_of(5, curve_recv).wait_recv()
     gathered = [curve_recv[d] for d in range(n_all)]
     while len(gathered) > 1:
         gathered = [
@@ -486,20 +485,21 @@
     interior_out[0, 0] = (
         interior_v[...].astype(jnp.float32) + step * extended_v[...]
     ).astype(jnp.bfloat16)
-    for off in range(1, n_sub):
-        group_arrival(3, off, image_send.at[off], image_recv).wait_recv()
+    all_of(3, image_recv).wait_recv()
     for k in range(slots):
         image = jnp.where(beside[k] >= 0, local_image[k] + partner(image_recv, k), 0.0)
         span = slice(k * LANES, (k + 1) * LANES)
         residual_out[0, 0, :, span] = residual[:, span] - step * image
 
-    for off in range(1, n_sub):
-        group_copy(0, off, basis_send.at[off], basis_recv).wait_send()
-        group_copy(1, off, slab_v, slab_recv).wait_send()
-        group_copy(2, off, solve_send.at[off], solve_recv).wait_send()
-        group_copy(3, off, image_send.at[off], image_recv).wait_send()
-    over_all(all_copy, lambda copy: copy.wait_send(), 0, packet_send, packet_recv)
-    over_all(all_copy, lambda copy: copy.wait_send(), 1, curve_send, curve_recv)
+    for kind, target in enumerate(
+        (basis_recv, slab_recv, solve_recv, image_recv, packet_recv, curve_recv)
+    ):
+        all_of(kind, target).wait_send()
+
+
+def handed_kernel(count, *refs):
+    for i in range(count):
+        refs[count + i][...] = refs[i][...]
 
 
 def fused(
@@ -528,9 +528,8 @@
     coarse = -(-coarse_count // LANES) * LANES
     face_total = coarse_count // (primal // slots) * (faces // slots)
     f32, bf16 = jnp.float32, jnp.bfloat16
-    smem = pl.BlockSpec(memory_space=pltpu.SMEM)
     vmem = pl.BlockSpec(memory_space=pltpu.VMEM)
-    far = pl.BlockSpec(memory_space=pl.ANY)
+    far = pl.BlockSpec(memory_space=pltpu.HBM)
     outs = pl.pallas_call(
         functools.partial(fused_kernel, n_grp, n_sub, float(face_total)),
         out_shape=[
@@ -540,15 +539,20 @@
             jax.ShapeDtypeStruct(interior.shape, bf16),
             jax.ShapeDtypeStruct((1, cases), f32),
         ],
-        in_specs=[smem, smem, smem, far, far, far, vmem, far, far, far, far, far, far, far],
+        in_specs=[far] * 14,
         out_specs=[vmem] * 5,
         scratch_shapes=[
+            pltpu.SMEM(neighbours.shape, jnp.int32),
+            pltpu.SMEM(coarse_rows.shape, jnp.int32),
+            pltpu.SMEM((1, 1) + extension_block_index.shape[:1:-1], jnp.int32),
+            pltpu.VMEM((1, cases), f32),
+            pltpu.VMEM((2, coarse, coarse + faces), bf16),
             pltpu.VMEM((cases, faces), f32),
             pltpu.VMEM((cases, faces), f32),
             pltpu.VMEM((cases, faces), f32),
             pltpu.VMEM((cases, interior_faces), bf16),
             pltpu.VMEM((1, faces), f32),
-            pltpu.VMEM((primal, faces), f32),
+            pltpu.VMEM((primal, 1, faces), f32),
             pltpu.VMEM((faces, faces), bf16),
             pltpu.VMEM((faces, faces), bf16),
             pltpu.VMEM(extension_values.shape[2:], bf16),
@@ -567,32 +571,37 @@
             pltpu.VMEM((n_sub, cases, LANES), f32),
             pltpu.VMEM((1, LANES), f32),
             pltpu.VMEM((n_all, 1, LANES), f32),
-            pltpu.SemaphoreType.DMA((10,)),
-            pltpu.SemaphoreType.DMA((4, n_sub)),
-            pltpu.SemaphoreType.DMA((4, n_sub)),
-            pltpu.SemaphoreType.DMA((2, n_all)),
-            pltpu.SemaphoreType.DMA((2, n_all)),
+            pltpu.SemaphoreType.DMA((14,)),
+            pltpu.SemaphoreType.DMA((6,)),
+            pltpu.SemaphoreType.DMA((6,)),
         ],
         compiler_params=pltpu.CompilerParams(
-            collective_id=0, has_side_effects=True, vmem_limit_bytes=24 * 1024 * 1024
+            collective_id=0, has_side_effects=True, vmem_limit_bytes=HELD_BYTES
         ),
     )(
         neighbours,
         coarse_rows,
-        extension_block_index,
+        jnp.swapaxes(extension_block_index, 2, 3),
         solution,
         residual,
         direction,
         inner_old.reshape(1, cases),
         interior,
         weights,
-        coarse_basis_matrix,
+        jnp.swapaxes(coarse_basis_matrix, 1, 2),
         local_solver,
         schur_matrix,
         extension_values,
         coarse_inverse,
     )
-    return (*outs[:4], outs[4].reshape(cases))
+    handed = pl.pallas_call(
+        functools.partial(handed_kernel, len(outs)),
+        out_shape=[jax.ShapeDtypeStruct(out.shape, out.dtype) for out in outs],
+        in_specs=[vmem] * len(outs),
+        out_specs=[vmem] * len(outs),
+        compiler_params=pltpu.CompilerParams(vmem_limit_bytes=HELD_BYTES),
+    )(*outs)
+    return (*handed[:4], handed[4].reshape(cases))
 
 
 def per_device(*arrays):

time: 36 us -> 24.2 us (0.67)
  local copies, waits for them, and re-layouts: 10 us -> 0 us
  Pallas kernels: 24.7 us -> 23.4 us
    unnamed x33 -> x0, local copies, waits for them, and re-layouts: 10 us -> none
    pallas_call x1, Pallas kernels: 24.7 us -> 21.9 us  [fused(): pl.pallas_call(functools.partial(fused_kernel, n_grp, n_sub, float(face_t...]
    pallas_call x0 -> x1, Pallas kernels: none -> 1.48 us  [fused(): pl.pallas_call(functools.partial(handed_kernel, len(outs)), out_shape=[ja...]
where the time goes in v2:
time: 24.2 us; the launch traced here: 24 us
  Pallas kernels  23.4 us (97%)
  between operations  0.65 us (3%)
    pallas_call x1, Pallas kernels, fused(): pl.pallas_call(functools.partial(fused_kernel, n_grp, n_sub, float(face_t...  21.9 us
    pallas_call x1, Pallas kernels, fused(): pl.pallas_call(functools.partial(handed_kernel, len(outs)), out_shape=[ja...  1.48 us

profile of v2, /device:TPU:0, one launch (start us, length us, event | category | flops | bytes accessed | tf_op | source)
XLA Modules:
  0.0 24.0 jit_solution(18152294369469121996)
XLA Ops:
  0.6 21.9 %shard_map.173 = (f32[1,1,16,512]{3,2,1,0:T(8,128)}, f32[1,1,16,512]{3,2,1,0:T(8,128)}, f32[1,1,16,512]{3,2,1,0:T(8,128)}, bf16[1,1,16,1536]{3,2,1,0:T(8,128)(2,1)}, f32[1,16]{1,0:T(1,128)}) custom-call(s32[1,1,4]{2,1,0:T(1,128)} %neighbours_in.1, s32[1,1,12]{2,1,0:T(1,128)} %rows_in.1, s32[1,1,2,12]{3,2,1,0:T(2,128)} %bitcast.5, ...), custom_call_target="tpu_custom_call" | custom-call | tf_op jit(solution)/shard_map/pallas_call | solution.py:533
  22.5 1.5 %shard_map.174 = (f32[1,1,16,512]{3,2,1,0:T(8,128)}, f32[1,1,16,512]{3,2,1,0:T(8,128)}, f32[1,1,16,512]{3,2,1,0:T(8,128)}, bf16[1,1,16,1536]{3,2,1,0:T(8,128)(2,1)}, f32[1,16]{1,0:T(1,128)}) custom-call(f32[1,1,16,512]{3,2,1,0:T(8,128)} %get-tuple-element.15.refs_0_, f32[1,1,16,512]{3,2,1,0:T(8,128)} %get-tuple-element.16.refs_1_, ...), custom_call_target="tpu_custom_call" | custom-call | tf_op jit(solution)/shard_map/pallas_call | solution.py:597

commit v3 on v2

--- a/solution.py
+++ b/solution.py
@@ -308,11 +308,6 @@
     locals_["slab"].wait()
     slab_recv[me_sub] = slab_v[...]
 
-    pl.semaphore_wait(barrier, n_all - 1)
-    for off in range(1, n_sub):
-        group_copy(0, off, basis_send.at[off], basis_recv).start()
-        group_copy(1, off, slab_v, slab_recv).start()
-
     locals_["solver"].wait()
     solve = jnp.dot(
         scaled.astype(jnp.bfloat16), solver_v[...], preferred_element_type=jnp.float32
@@ -331,8 +326,12 @@
     )
     packet_send[...] = packet
     packet_recv[me] = packet
+    pl.semaphore_wait(barrier, n_all - 1)
     for peer in everyone:
         all_copy(4, peer, packet_send, packet_recv).start()
+    for off in range(1, n_sub):
+        group_copy(0, off, basis_send.at[off], basis_recv).start()
+        group_copy(1, off, slab_v, slab_recv).start()
     weighted_solve = cut(weight * solve)
     for off in range(1, n_sub):
         solve_send[off] = routed(off, weighted_solve)
@@ -438,9 +437,6 @@
     local_image = cut(
         jnp.dot(direction_half, schur_v[...], preferred_element_type=jnp.float32)
     )
-    for off in range(1, n_sub):
-        image_send[off] = routed(off, local_image)
-        group_copy(3, off, image_send.at[off], image_recv).start()
     bent = None
     for k in range(slots):
         term = jnp.where(beside[k] >= 0, news[k] * local_image[k], 0.0)
@@ -451,6 +447,9 @@
     curve_recv[me] = bent_row
     for peer in everyone:
         all_copy(5, peer, curve_send, curve_recv).start()
+    for off in range(1, n_sub):
+        image_send[off] = routed(off, local_image)
+        group_copy(3, off, image_send.at[off], image_recv).start()
 
     direction_out[0, 0] = direction_new
     for k in range(slots):

time: 24.2 us -> 22.3 us (0.921)
  Pallas kernels: 23.4 us -> 21.4 us
    pallas_call x1, Pallas kernels: 21.9 us -> 19.9 us  [fused(): pl.pallas_call(functools.partial(fused_kernel, n_grp, n_sub, float(face_t...]
where the time goes in v3:
time: 22.3 us; the launch traced here: 22.1 us
  Pallas kernels  21.4 us (96%)
  between operations  0.65 us (3%)
    pallas_call x1, Pallas kernels, fused(): pl.pallas_call(functools.partial(fused_kernel, n_grp, n_sub, float(face_t...  19.9 us
    pallas_call x1, Pallas kernels, fused(): pl.pallas_call(functools.partial(handed_kernel, len(outs)), out_shape=[ja...  1.48 us

profile of v3, /device:TPU:0, one launch (start us, length us, event | category | flops | bytes accessed | tf_op | source)
XLA Modules:
  0.0 22.1 jit_solution(17454478105200184197)
XLA Ops:
  0.6 19.9 %shard_map.173 = (f32[1,1,16,512]{3,2,1,0:T(8,128)}, f32[1,1,16,512]{3,2,1,0:T(8,128)}, f32[1,1,16,512]{3,2,1,0:T(8,128)}, bf16[1,1,16,1536]{3,2,1,0:T(8,128)(2,1)}, f32[1,16]{1,0:T(1,128)}) custom-call(s32[1,1,4]{2,1,0:T(1,128)} %neighbours_in.1, s32[1,1,12]{2,1,0:T(1,128)} %rows_in.1, s32[1,1,2,12]{3,2,1,0:T(2,128)} %bitcast.5, ...), custom_call_target="tpu_custom_call" | custom-call | tf_op jit(solution)/shard_map/pallas_call | solution.py:532
  20.6 1.5 %shard_map.174 = (f32[1,1,16,512]{3,2,1,0:T(8,128)}, f32[1,1,16,512]{3,2,1,0:T(8,128)}, f32[1,1,16,512]{3,2,1,0:T(8,128)}, bf16[1,1,16,1536]{3,2,1,0:T(8,128)(2,1)}, f32[1,16]{1,0:T(1,128)}) custom-call(f32[1,1,16,512]{3,2,1,0:T(8,128)} %get-tuple-element.15.refs_0_, f32[1,1,16,512]{3,2,1,0:T(8,128)} %get-tuple-element.16.refs_1_, ...), custom_call_target="tpu_custom_call" | custom-call | tf_op jit(solution)/shard_map/pallas_call | solution.py:596
